TPU v7x, 256 devices: a whole 4x4x8 slice. The times are simulated.
256 devices in a mesh: seq: 32 (over x, y, z_lo), chan: 8 (over z_hi, core).
Axes of the slice: x: 4, y: 4, z: 8 (z_hi: 4, z_lo: 2; z = z_hi * 2 + z_lo), core: 2. Of those that a mesh axis runs over, the one named last changes fastest.
Arguments:
- value: bfloat16 [32768, 2048], P('seq', 'chan'), may hold values from -6 to 6
- gate_in: bfloat16 [32768, 2048], P('seq', 'chan'), may hold values from -6 to 6
- gate_out: bfloat16 [32768, 2048], P('seq', 'chan'), may hold values from -6 to 6
- skip_weight: float32 [2048], P('chan'), may hold values from -1 to 1
- spectrum: float32 [2, 512, 128, 2048], P(None, 'seq', None, 'chan'), may hold values from -6 to 6
- out_weight: bfloat16 [2048, 2048], P('chan'), may hold values from -0.125 to 0.125
Outputs:
- projected: bfloat16 [32768, 2048], P(('seq', 'chan'))
All inputs are finite; a program needn't handle non-finite values.
Results may differ from a plain program's by a relative error of at most 0.0057.
Values may be sent and summed in bfloat16 or wider, within the bound.
A program may use at most 128 MiB of HBM per device.

v0:
```python
import functools
import math

import jax
import jax.numpy as jnp
import ml_dtypes
import numpy as np
from jax import lax
from jax.experimental import pallas as pl
from jax.experimental.pallas import tpu as pltpu
from jax.sharding import PartitionSpec as P

COLS = 128
LANE = 128
CH = 8
BAND = 16
GROUP = 8
MESH = pl.DeviceIdType.MESH
F32 = jnp.float32
BF16 = jnp.bfloat16


def two_terms(matrix):
    high = matrix.astype(np.float32).astype(ml_dtypes.bfloat16)
    low = (matrix - high.astype(np.float64)).astype(np.float32).astype(ml_dtypes.bfloat16)
    return np.stack([high, low])


def constants(seq_size):
    half_rows = 8 * seq_size
    row_count = 2 * half_rows
    padded_len = row_count * COLS
    k1 = np.arange(row_count)
    a = np.arange(half_rows)
    b = np.arange(COLS)
    row = 2.0 * np.pi / row_count * (np.outer(k1, a) % row_count)
    fwd_row = np.concatenate([np.cos(row), -np.sin(row)], axis=0)
    twist = 2.0 * np.pi / padded_len * (np.outer(k1, b) % padded_len)
    turn = np.stack([np.cos(twist), np.sin(twist)]).astype(np.float32)
    col = 2.0 * np.pi / COLS * (np.outer(b, b) % COLS)
    cos, sin = np.cos(col), np.sin(col)
    fwd_col = np.block([[cos, -sin], [sin, cos]])
    inv_col = np.block([[cos, sin], [-sin, cos]])
    groups = seq_size // min(GROUP, seq_size)
    back = row.T.reshape(half_rows, groups, -1)
    inv_row = np.concatenate([np.cos(back), -np.sin(back)], axis=2) / padded_len
    inv_row = np.ascontiguousarray(inv_row.transpose(1, 0, 2))
    return two_terms(fwd_row), turn, two_terms(fwd_col), two_terms(inv_col), two_terms(inv_row)


def mm(x, y):
    return jnp.dot(x, y, preferred_element_type=F32)


def conv_kernel(
    seq_size,
    chan_size,
    value,
    gate_in,
    gate_out,
    skip,
    spectrum,
    fwd_row_hbm,
    turn_hbm,
    fwd_col_hbm,
    inv_col_hbm,
    inv_row_hbm,
    out,
    fwd_row,
    turn,
    fwd_col,
    inv_col,
    inv_row,
    gate_buf,
    spec_buf,
    xsend,
    xrecv,
    xwide,
    xgrid,
    hwide,
    hsend,
    hrecv,
    freq,
    back,
    total,
    ysend,
    yrecv,
    ywide,
    gate_t,
    gsend,
    load_sem,
    spec_sem,
    xs,
    xr,
    hs,
    hr,
    ys,
    yr,
    gs,
    gr,
):
    me = lax.axis_index("seq")
    mc = lax.axis_index("chan")
    half_rows = 8 * seq_size
    width = CH * seq_size
    members = min(GROUP, seq_size)
    groups = seq_size // members
    krows = members * BAND

    loads = [
        pltpu.make_async_copy(fwd_row_hbm, fwd_row, load_sem.at[0]),
        pltpu.make_async_copy(turn_hbm, turn, load_sem.at[1]),
        pltpu.make_async_copy(fwd_col_hbm, fwd_col, load_sem.at[2]),
        pltpu.make_async_copy(inv_col_hbm, inv_col, load_sem.at[3]),
        pltpu.make_async_copy(inv_row_hbm, inv_row, load_sem.at[4]),
        pltpu.make_async_copy(gate_out, gate_buf, load_sem.at[5]),
    ]
    spec_loads = [
        pltpu.make_async_copy(spectrum.at[part], spec_buf.at[part], spec_sem.at[part])
        for part in range(2)
    ]
    for copy in spec_loads + loads:
        copy.start()

    barrier = pltpu.get_barrier_semaphore()

    def greet_seq(d, _):
        peer = lax.rem(me + d, seq_size)
        pl.semaphore_signal(barrier, inc=1, device_id=(peer, mc), device_id_type=MESH)
        return 0

    def greet_chan(d, _):
        peer = lax.rem(mc + d, chan_size)
        pl.semaphore_signal(barrier, inc=1, device_id=(me, peer), device_id_type=MESH)
        return 0

    lax.fori_loop(1, seq_size, greet_seq, 0)
    lax.fori_loop(1, chan_size, greet_chan, 0)

    def exchange(src_of, dst, send_sem, recv_sem):
        own = pltpu.make_async_copy(src_of(me), dst, recv_sem)
        own.start()

        def send(d, _):
            peer = lax.rem(me + d, seq_size)
            pltpu.make_async_remote_copy(
                src_ref=src_of(peer),
                dst_ref=dst,
                send_sem=send_sem,
                recv_sem=recv_sem,
                device_id=(peer, mc),
                device_id_type=MESH,
            ).start()
            return 0

        lax.fori_loop(1, seq_size, send, 0)

    for pair in range(4):
        halves = []
        for a in (2 * pair, 2 * pair + 1):
            rows = slice(a * COLS, (a + 1) * COLS)
            mixed = (gate_in[rows, :].astype(F32) * value[rows, :].astype(F32)).astype(BF16)
            halves.append(mixed.astype(F32).T.reshape(seq_size, CH, LANE))
        xsend[:, pair * 16 : (pair + 1) * 16, :] = jnp.concatenate(halves, axis=1).astype(BF16)

    pl.semaphore_wait(barrier, seq_size - 1 + chan_size - 1)
    exchange(lambda peer: xsend.at[peer], xrecv.at[me], xs, xr)

    for part in range(2):
        spec_loads[part].wait()

        def turn_row(k, _):
            start = pl.multiple_of(k * width, width)
            hwide[pl.ds(start, width), :] = spec_buf[part, k].T
            return 0

        lax.fori_loop(0, BAND, turn_row, 0)

        def pack(dest, _):
            for c in range(CH):
                rows = hwide[pl.ds(dest * CH + c, BAND, stride=width), :]
                hsend[part, dest, c * BAND : (c + 1) * BAND, :] = rows.astype(BF16)
            return 0

        lax.fori_loop(0, seq_size, pack, 0)
        exchange(
            lambda peer: hsend.at[part, peer],
            hrecv.at[part, me],
            hs.at[part],
            hr.at[part, me // members],
        )

    loads[5].wait()
    for a in range(8):
        gate_t[a] = gate_buf[a * COLS : (a + 1) * COLS, :].astype(F32).T.astype(BF16)

    for copy in loads[:5]:
        copy.wait()
    pltpu.make_async_copy(xsend, xrecv, xr).wait()
    xwide[...] = xrecv[...].astype(F32).reshape(seq_size * 64, LANE)
    for c in range(CH):
        xgrid[:, c * LANE : (c + 1) * LANE] = xwide[pl.ds(c, half_rows, stride=CH), :].astype(BF16)

    row_count = 2 * half_rows

    def forward(g, _):
        rows = pl.ds(pl.multiple_of(g * krows, krows), krows)
        rows_im = pl.ds(pl.multiple_of(row_count + g * krows, krows), krows)
        cos, sin = turn[0, rows, :], turn[1, rows, :]
        for pair in range(CH // 2):
            x = xgrid[:, pair * 256 : (pair + 1) * 256]
            re = mm(fwd_row[0, rows, :], x) + mm(fwd_row[1, rows, :], x)
            im = mm(fwd_row[0, rows_im, :], x) + mm(fwd_row[1, rows_im, :], x)
            for h in range(2):
                r = re[:, h * LANE : (h + 1) * LANE]
                i = im[:, h * LANE : (h + 1) * LANE]
                turned = jnp.concatenate([r * cos + i * sin, i * cos - r * sin], axis=1)
                high = turned.astype(BF16)
                low = (turned - high.astype(F32)).astype(BF16)
                freq[2 * pair + h, rows, :] = (
                    mm(high, fwd_col[0]) + mm(high, fwd_col[1]) + mm(low, fwd_col[0])
                )
        return 0

    lax.fori_loop(0, groups, forward, 0)

    total[...] = jnp.zeros_like(total)
    def inverse(g, _):
        members_at = pl.ds(pl.multiple_of(g * members, members), members)
        for part in range(2):
            block = hrecv.at[part, members_at]
            pltpu.make_async_copy(hsend.at[part, members_at], block, hr.at[part, g]).wait()
        rows = pl.ds(pl.multiple_of(g * krows, krows), krows)
        cos, sin = turn[0, rows, :], turn[1, rows, :]
        for c in range(CH):
            band = slice(c * BAND, (c + 1) * BAND)
            h_re = hrecv[0, members_at, band, :].astype(F32).reshape(krows, LANE)
            h_im = hrecv[1, members_at, band, :].astype(F32).reshape(krows, LANE)
            f_re, f_im = freq[c, rows, :LANE], freq[c, rows, LANE:]
            prod = jnp.concatenate([f_re * h_re - f_im * h_im, f_re * h_im + f_im * h_re], axis=1)
            prod = prod.astype(BF16)
            grid = mm(prod, inv_col[0]) + mm(prod, inv_col[1])
            b_re, b_im = grid[:, :LANE], grid[:, LANE:]
            lanes = slice(c * LANE, (c + 1) * LANE)
            back[:krows, lanes] = (b_re * cos - b_im * sin).astype(BF16)
            back[krows:, lanes] = (b_re * sin + b_im * cos).astype(BF16)
        for pair in range(CH // 2):
            lanes = slice(pair * 256, (pair + 1) * 256)
            total[:, lanes] += mm(inv_row[0, g], back[:, lanes]) + mm(inv_row[1, g], back[:, lanes])
        return 0

    lax.fori_loop(0, groups, inverse, 0)

    weights = skip[me]
    for pair in range(CH // 2):
        halves = []
        for c in (2 * pair, 2 * pair + 1):
            lanes = slice(c * LANE, (c + 1) * LANE)
            inner = total[:, lanes] + weights[c : c + 1, :] * xgrid[:, lanes].astype(F32)
            halves.append(inner.reshape(seq_size, 8, LANE))
        ysend[:, pair * 16 : (pair + 1) * 16, :] = jnp.concatenate(halves, axis=1).astype(BF16)
    exchange(lambda peer: ysend.at[peer], yrecv.at[me], ys, yr)
    pltpu.make_async_copy(ysend, yrecv, yr).wait()
    ywide[...] = yrecv[...].astype(F32).reshape(seq_size * 64, LANE)
    for a in range(8):
        inner = ywide[pl.ds(a, width, stride=8), :]
        gsend[a] = (gate_t[a].astype(F32) * inner).astype(BF16)

    own = pltpu.make_async_copy(gsend.at[mc], out.at[mc], gr)
    own.start()

    def send(d, _):
        peer = lax.rem(mc + d, chan_size)
        pltpu.make_async_remote_copy(
            src_ref=gsend.at[peer],
            dst_ref=out.at[mc],
            send_sem=gs,
            recv_sem=gr,
            device_id=(me, peer),
            device_id_type=MESH,
        ).start()
        return 0

    lax.fori_loop(1, chan_size, send, 0)
    pltpu.make_async_copy(gsend, out, gr).wait()

    others = pl.ds(0, seq_size - 1)
    pltpu.make_async_copy(xsend.at[others], xrecv.at[others], xs).wait()
    for part in range(2):
        pltpu.make_async_copy(hsend.at[part, others], hrecv.at[part, others], hs.at[part]).wait()
    pltpu.make_async_copy(ysend.at[others], yrecv.at[others], ys).wait()
    rest = pl.ds(0, chan_size - 1)
    pltpu.make_async_copy(gsend.at[rest], out.at[rest], gs).wait()


def long_conv(seq_size, chan_size, value, gate_in, gate_out, skip_weight, spectrum):
    half_rows = 8 * seq_size
    row_count = 2 * half_rows
    width = CH * seq_size
    members = min(GROUP, seq_size)
    groups = seq_size // members
    krows = members * BAND
    mats = constants(seq_size)
    skip = jnp.broadcast_to(skip_weight.reshape(seq_size, CH, 1), (seq_size, CH, LANE))
    vmem = pl.BlockSpec(memory_space=pltpu.VMEM)
    hbm = pl.BlockSpec(memory_space=pl.ANY)
    dma = pltpu.SemaphoreType.DMA
    return pl.pallas_call(
        functools.partial(conv_kernel, seq_size, chan_size),
        out_shape=jax.ShapeDtypeStruct((chan_size, width, LANE), BF16),
        in_specs=[vmem, vmem, hbm, vmem, hbm] + [hbm] * 5,
        out_specs=hbm,
        scratch_shapes=[
            *[pltpu.VMEM(m.shape, F32 if m.dtype == np.float32 else BF16) for m in mats],
            pltpu.VMEM((1024, width), BF16),
            pltpu.VMEM((2, BAND, COLS, width), F32),
            pltpu.VMEM((seq_size, 64, LANE), BF16),
            pltpu.VMEM((seq_size, 64, LANE), BF16),
            pltpu.VMEM((seq_size * 64, LANE), F32),
            pltpu.VMEM((half_rows, CH * LANE), BF16),
            pltpu.VMEM((BAND * width, LANE), F32),
            pltpu.VMEM((2, seq_size, CH * BAND, LANE), BF16),
            pltpu.VMEM((2, seq_size, CH * BAND, LANE), BF16),
            pltpu.VMEM((CH, row_count, 2 * LANE), F32),
            pltpu.VMEM((2 * krows, CH * LANE), BF16),
            pltpu.VMEM((half_rows, CH * LANE), F32),
            pltpu.VMEM((seq_size, 64, LANE), BF16),
            pltpu.VMEM((seq_size, 64, LANE), BF16),
            pltpu.VMEM((seq_size * 64, LANE), F32),
            pltpu.VMEM((8, width, LANE), BF16),
            pltpu.VMEM((8, width, LANE), BF16),
            dma((6,)),
            dma((2,)),
            dma,
            dma,
            dma((2,)),
            dma((2, groups)),
            dma,
            dma,
            dma,
            dma,
        ],
        compiler_params=pltpu.CompilerParams(
            collective_id=0, has_side_effects=True, vmem_limit_bytes=50 * 1024 * 1024
        ),
        name="long_conv",
    )(value, gate_in, gate_out, skip, spectrum, *[jnp.asarray(m) for m in mats])


def local(value, gate_in, gate_out, skip_weight, spectrum, out_weight):
    seq_size = lax.axis_size("seq")
    chan_size = lax.axis_size("chan")
    weight = lax.all_gather(out_weight, "chan", axis=0, tiled=True)
    gated = long_conv(seq_size, chan_size, value, gate_in, gate_out, skip_weight, spectrum)
    gated = gated.reshape(-1, LANE)
    out = lax.dot_general(gated, weight, (((0,), (0,)), ((), ())), preferred_element_type=F32)
    return out.astype(BF16)


def solution(mesh):
    placed = (
        P("seq", "chan"),
        P("seq", "chan"),
        P("seq", "chan"),
        P("chan"),
        P(None, "seq", None, "chan"),
        P("chan", None),
    )
    return jax.shard_map(
        local, mesh=mesh, in_specs=placed, out_specs=P(("seq", "chan"), None), check_vma=False
    )
```

profile of v0, /device:TPU:1, one launch (start us, length us, event | category | flops | bytes accessed | tf_op | source)
XLA Modules:
  0.0 153.5 jit_solution(12680481193961934787)
XLA Ops:
  6.5 0.0 all-gather.2.cloned.1.call-start
  6.5 0.7 all-gather.2.cloned.1.call-update
  7.3 0.8 broadcast_in_dim.7
  8.0 0.1 broadcast_in_dim.8.skip
  8.1 0.0 copy-start
  8.1 1.0 copy-done
  9.2 0.0 copy-start.1
  9.2 1.0 copy-done.1
  10.2 0.0 copy-start.2
  10.2 1.0 copy-done.2
  11.3 0.0 copy-start.3
  11.3 1.0 copy-done.3
  12.3 0.0 copy-start.4
  12.3 0.9 copy-done.4
  13.2 0.0 copy-start.5
  13.2 0.9 copy-done.5
  14.2 127.0 %long_conv.1 = bf16[8,256,128]{2,1,0:T(8,128)(2,1)S(1)} custom-call(bf16[1024,256]{1,0:T(8,128)(2,1)S(1)} %copy-done, bf16[1024,256]{1,0:T(8,128)(2,1)S(1)} %copy-done.1, bf16[1024,256]{1,0:T(8,128)(2,1)S(1)} %copy-done.2, f32[32,8,128]{2,1,0:T(8,128)S(1)} %broadcast_in_dim.8.skip, f32[2,16,128,256]{3,2,1,0:T(8,128)} %spectrum.1, ...), custom_call_target="tpu_custom_call" | custom-call | tf_op jit(solution)/shard_map/long_conv/pallas_call | solution.py:308
  141.2 0.0 all-gather.2.cloned.1.call-done
  141.2 5.5 %convolution_convert_fusion = bf16[128,2048]{1,0:T(8,128)(2,1)} fusion(bf16[2048,128]{1,0:T(8,128)(2,1)S(1)} %bitcast.3, bf16[2048,2048]{1,0:T(8,128)(2,1)} %all-gather.2.cloned.1.call-done), kind=kOutput, calls=%fused_computation | convolution fusion | flops 1074003968 | bytes 9437184 | tf_op jit(solution)/shard_map/dot_general | solution.py:356
Async XLA Ops:
  6.5 134.7 %all-gather.2.cloned.1.call-start = ((), (), s32[]{:S(2)}) async-start(), calls=%async_computation | async-start | bytes 9437184 | tf_op jit(solution)/shard_map/all_gather | solution.py:353
  8.1 1.0 copy-start
  9.2 1.0 copy-start.1
  10.2 1.0 copy-start.2
  11.3 1.0 copy-start.3
  12.3 0.9 copy-start.4
  13.2 0.9 copy-start.5
Sparse Core Ops, SparseCore 0:
  9.2 122.8 all-gather.1
where the time goes:
time: 154 us
  Pallas kernels  127 us (82%)
  between operations  13.4 us (9%)
  local copies, waits for them, and re-layouts  6.92 us (4%)
  matrix products  5.46 us (4%)
    pallas_call x1, Pallas kernels, long_conv(): pl.pallas_call(functools.partial(conv_kernel, seq_size, chan_size), out_s...  127 us
    unnamed x12, local copies, waits for them, and re-layouts  6.06 us
    dot_general x1, matrix products, local(): lax.dot_general(gated, weight, (((0,), (0,)), ((), ())), preferred_elemen...  5.46 us
  transfers between devices with their start and end apart: 1, of which 0 were waited for; matrix products, arithmetic and copies ran while one was open for 1% of the time, Pallas kernels for 83%

commit v1 on v0

--- a/solution.py
+++ b/solution.py
@@ -15,6 +15,8 @@
 CH = 8
 BAND = 16
 GROUP = 8
+NODES = 4
+SPANS, SPAN = 4, 512
 MESH = pl.DeviceIdType.MESH
 F32 = jnp.float32
 BF16 = jnp.bfloat16
@@ -54,12 +56,12 @@
 
 def conv_kernel(
     seq_size,
-    chan_size,
-    value,
-    gate_in,
-    gate_out,
+    value_hbm,
+    gate_in_hbm,
+    gate_out_hbm,
     skip,
     spectrum,
+    weight_hbm,
     fwd_row_hbm,
     turn_hbm,
     fwd_col_hbm,
@@ -71,8 +73,11 @@
     fwd_col,
     inv_col,
     inv_row,
-    gate_buf,
+    value,
+    gate_in,
+    gate_out,
     spec_buf,
+    weight,
     xsend,
     xrecv,
     xwide,
@@ -86,8 +91,10 @@
     ysend,
     yrecv,
     ywide,
-    gate_t,
     gsend,
+    grecv,
+    partial,
+    mate_part,
     load_sem,
     spec_sem,
     xs,
@@ -98,63 +105,117 @@
     yr,
     gs,
     gr,
+    ws,
+    wr,
+    es,
+    er,
+    ms,
+    mr,
 ):
     me = lax.axis_index("seq")
     mc = lax.axis_index("chan")
     half_rows = 8 * seq_size
+    row_count = 2 * half_rows
     width = CH * seq_size
-    members = min(GROUP, seq_size)
+    members = GROUP
     groups = seq_size // members
     krows = members * BAND
-
+    px, py, low = me // 8, lax.rem(me // 2, 4), lax.rem(me, 2)
+    node, core = mc // 2, lax.rem(mc, 2)
+    pair_chip = me + 1 - 2 * low
+    near = lax.rem(node + 3 + 2 * low, NODES)
+    far = lax.rem(node + 5 - 2 * low, NODES)
+    across = lax.rem(node + 2, NODES)
+    mine = lax.rem(px + py, 2)
+    beside = [
+        lax.rem(px + 1, 4) * 8 + py * 2 + low,
+        lax.rem(px + 3, 4) * 8 + py * 2 + low,
+        px * 8 + lax.rem(py + 1, 4) * 2 + low,
+        px * 8 + lax.rem(py + 3, 4) * 2 + low,
+    ]
+
+    def remote(src, dst, send_sem, recv_sem, seq, chan):
+        return pltpu.make_async_remote_copy(
+            src_ref=src,
+            dst_ref=dst,
+            send_sem=send_sem,
+            recv_sem=recv_sem,
+            device_id=(seq, chan),
+            device_id_type=MESH,
+        )
+
+    mixed_loads = [
+        pltpu.make_async_copy(value_hbm, value, load_sem.at[6]),
+        pltpu.make_async_copy(gate_in_hbm, gate_in, load_sem.at[7]),
+    ]
+    weight_load = pltpu.make_async_copy(weight_hbm, weight.at[node], load_sem.at[8])
     loads = [
         pltpu.make_async_copy(fwd_row_hbm, fwd_row, load_sem.at[0]),
         pltpu.make_async_copy(turn_hbm, turn, load_sem.at[1]),
         pltpu.make_async_copy(fwd_col_hbm, fwd_col, load_sem.at[2]),
         pltpu.make_async_copy(inv_col_hbm, inv_col, load_sem.at[3]),
         pltpu.make_async_copy(inv_row_hbm, inv_row, load_sem.at[4]),
-        pltpu.make_async_copy(gate_out, gate_buf, load_sem.at[5]),
+        pltpu.make_async_copy(gate_out_hbm, gate_out, load_sem.at[5]),
     ]
     spec_loads = [
         pltpu.make_async_copy(spectrum.at[part], spec_buf.at[part], spec_sem.at[part])
         for part in range(2)
     ]
-    for copy in spec_loads + loads:
+    for copy in mixed_loads + [weight_load] + spec_loads + loads:
         copy.start()
 
     barrier = pltpu.get_barrier_semaphore()
 
+    def greet(seq, chan):
+        pl.semaphore_signal(barrier, inc=1, device_id=(seq, chan), device_id_type=MESH)
+
     def greet_seq(d, _):
-        peer = lax.rem(me + d, seq_size)
-        pl.semaphore_signal(barrier, inc=1, device_id=(peer, mc), device_id_type=MESH)
+        greet(lax.rem(me + d, seq_size), mc)
         return 0
 
-    def greet_chan(d, _):
-        peer = lax.rem(mc + d, chan_size)
-        pl.semaphore_signal(barrier, inc=1, device_id=(me, peer), device_id_type=MESH)
-        return 0
-
     lax.fori_loop(1, seq_size, greet_seq, 0)
-    lax.fori_loop(1, chan_size, greet_chan, 0)
+    greet(me, mc + 1 - 2 * core)
+    greet(pair_chip, near * 2 + core)
+    for step in range(1, NODES):
+        greet(me, lax.rem(node + step, NODES) * 2 + core)
 
     def exchange(src_of, dst, send_sem, recv_sem):
-        own = pltpu.make_async_copy(src_of(me), dst, recv_sem)
-        own.start()
+        pltpu.make_async_copy(src_of(me), dst, recv_sem).start()
 
         def send(d, _):
-            peer = lax.rem(me + d, seq_size)
-            pltpu.make_async_remote_copy(
-                src_ref=src_of(peer),
-                dst_ref=dst,
-                send_sem=send_sem,
-                recv_sem=recv_sem,
-                device_id=(peer, mc),
-                device_id_type=MESH,
-            ).start()
+            peer = (
+                lax.rem(px + d // 8, 4) * 8
+                + lax.rem(py + lax.rem(d // 2, 4), 4) * 2
+                + lax.rem(low + d, 2)
+            )
+            remote(src_of(peer), dst, send_sem, recv_sem, peer, mc).start()
             return 0
 
         lax.fori_loop(1, seq_size, send, 0)
 
+    def pass_near():
+        block = weight.at[node, mine]
+        return remote(block, block, ws.at[0], wr.at[0], pair_chip, near * 2 + core)
+
+    def pass_pair():
+        block = weight.at[near, mine]
+        return remote(block, block, ws.at[1], wr.at[1], pair_chip, mc)
+
+    def pass_across():
+        block = weight.at[far, mine, pl.ds(pl.multiple_of(low * 64, 64), 64)]
+        return remote(block, block, ws.at[2], wr.at[2], pair_chip, near * 2 + core)
+
+    def pass_across_pair():
+        block = weight.at[across, mine, pl.ds(pl.multiple_of(64 - low * 64, 64), 64)]
+        return remote(block, block, ws.at[3], wr.at[3], pair_chip, mc)
+
+    def pass_beside(slot, which):
+        for e, seq in enumerate(beside):
+            block = weight.at[which, mine, pl.ds(e * 32, 32)]
+            remote(block, block, es.at[slot], er.at[slot], seq, mc).start()
+
+    for copy in mixed_loads:
+        copy.wait()
     for pair in range(4):
         halves = []
         for a in (2 * pair, 2 * pair + 1):
@@ -163,7 +224,9 @@
             halves.append(mixed.astype(F32).T.reshape(seq_size, CH, LANE))
         xsend[:, pair * 16 : (pair + 1) * 16, :] = jnp.concatenate(halves, axis=1).astype(BF16)
 
-    pl.semaphore_wait(barrier, seq_size - 1 + chan_size - 1)
+    weight_load.wait()
+    pl.semaphore_wait(barrier, seq_size - 1 + 5)
+    pass_near().start()
     exchange(lambda peer: xsend.at[peer], xrecv.at[me], xs, xr)
 
     for part in range(2):
@@ -187,21 +250,17 @@
             lambda peer: hsend.at[part, peer],
             hrecv.at[part, me],
             hs.at[part],
-            hr.at[part, me // members],
+            hr.at[part, px],
         )
 
-    loads[5].wait()
-    for a in range(8):
-        gate_t[a] = gate_buf[a * COLS : (a + 1) * COLS, :].astype(F32).T.astype(BF16)
-
-    for copy in loads[:5]:
+    for copy in loads:
         copy.wait()
     pltpu.make_async_copy(xsend, xrecv, xr).wait()
+    pass_near().wait_recv()
+    pass_pair().start()
     xwide[...] = xrecv[...].astype(F32).reshape(seq_size * 64, LANE)
     for c in range(CH):
         xgrid[:, c * LANE : (c + 1) * LANE] = xwide[pl.ds(c, half_rows, stride=CH), :].astype(BF16)
-
-    row_count = 2 * half_rows
 
     def forward(g, _):
         rows = pl.ds(pl.multiple_of(g * krows, krows), krows)
@@ -216,16 +275,22 @@
                 i = im[:, h * LANE : (h + 1) * LANE]
                 turned = jnp.concatenate([r * cos + i * sin, i * cos - r * sin], axis=1)
                 high = turned.astype(BF16)
-                low = (turned - high.astype(F32)).astype(BF16)
+                rest = (turned - high.astype(F32)).astype(BF16)
                 freq[2 * pair + h, rows, :] = (
-                    mm(high, fwd_col[0]) + mm(high, fwd_col[1]) + mm(low, fwd_col[0])
+                    mm(high, fwd_col[0]) + mm(high, fwd_col[1]) + mm(rest, fwd_col[0])
                 )
         return 0
 
     lax.fori_loop(0, groups, forward, 0)
+    pass_pair().wait_recv()
+    pass_across().start()
+    pass_beside(0, near)
+    pass_beside(1, far)
 
     total[...] = jnp.zeros_like(total)
-    def inverse(g, _):
+
+    def inverse(step, _):
+        g = lax.rem(px + groups - step, groups)
         members_at = pl.ds(pl.multiple_of(g * members, members), members)
         for part in range(2):
             block = hrecv.at[part, members_at]
@@ -249,71 +314,106 @@
             total[:, lanes] += mm(inv_row[0, g], back[:, lanes]) + mm(inv_row[1, g], back[:, lanes])
         return 0
 
-    lax.fori_loop(0, groups, inverse, 0)
-
-    weights = skip[me]
+    lax.fori_loop(0, groups - 1, inverse, 0)
+    pass_across().wait_recv()
+    pass_across_pair().start()
+    inverse(groups - 1, 0)
+
     for pair in range(CH // 2):
         halves = []
         for c in (2 * pair, 2 * pair + 1):
             lanes = slice(c * LANE, (c + 1) * LANE)
-            inner = total[:, lanes] + weights[c : c + 1, :] * xgrid[:, lanes].astype(F32)
+            inner = total[:, lanes] + skip[me * CH + c] * xgrid[:, lanes].astype(F32)
             halves.append(inner.reshape(seq_size, 8, LANE))
         ysend[:, pair * 16 : (pair + 1) * 16, :] = jnp.concatenate(halves, axis=1).astype(BF16)
     exchange(lambda peer: ysend.at[peer], yrecv.at[me], ys, yr)
+    pass_across_pair().wait_recv()
+    pass_beside(2, across)
     pltpu.make_async_copy(ysend, yrecv, yr).wait()
     ywide[...] = yrecv[...].astype(F32).reshape(seq_size * 64, LANE)
-    for a in range(8):
-        inner = ywide[pl.ds(a, width, stride=8), :]
-        gsend[a] = (gate_t[a].astype(F32) * inner).astype(BF16)
-
-    own = pltpu.make_async_copy(gsend.at[mc], out.at[mc], gr)
-    own.start()
-
-    def send(d, _):
-        peer = lax.rem(mc + d, chan_size)
-        pltpu.make_async_remote_copy(
-            src_ref=gsend.at[peer],
-            dst_ref=out.at[mc],
-            send_sem=gs,
-            recv_sem=gr,
-            device_id=(me, peer),
-            device_id_type=MESH,
-        ).start()
-        return 0
-
-    lax.fori_loop(1, chan_size, send, 0)
-    pltpu.make_async_copy(gsend, out, gr).wait()
+
+    for step in (2, 1, 3, 0):
+        dest = lax.rem(node + step, NODES)
+        for h in range(2):
+            a = dest * 2 + h
+            inner = ywide[pl.ds(a, width, stride=8), :].T
+            gate = gate_out[pl.ds(pl.multiple_of(a * COLS, COLS), COLS), :]
+            gsend[dest, h] = (gate.astype(F32) * inner).astype(BF16)
+        if step:
+            remote(
+                gsend.at[dest], grecv.at[node], gs.at[step], gr.at[node], me, dest * 2 + core
+            ).start()
+
+    def product(rows_of, which, n):
+        rows = rows_of.reshape(2 * COLS, width)
+        lanes = slice(n * SPAN, (n + 1) * SPAN)
+        return mm(rows, weight[which, :, :, lanes].reshape(width, SPAN)).reshape(2, COLS, SPAN)
+
+    for n in range(SPANS):
+        partial[n] = product(gsend[node], node, n)
+    for slot, which in enumerate((near, far, across)):
+        pltpu.make_async_copy(gsend.at[which], grecv.at[which], gr.at[which]).wait()
+        half = weight.at[which, 1 - mine]
+        pltpu.make_async_copy(half, half, er.at[slot]).wait()
+        rows = grecv[which]
+        for n in range(SPANS):
+            partial[n] += product(rows, which, n)
+            if slot == 2:
+                remote(
+                    partial.at[n, 1 - core],
+                    mate_part.at[n],
+                    ms.at[n],
+                    mr.at[n],
+                    me,
+                    mc + 1 - 2 * core,
+                ).start()
+    for n in range(SPANS):
+        pltpu.make_async_copy(mate_part.at[n], mate_part.at[n], mr.at[n]).wait()
+        out[:, n * SPAN : (n + 1) * SPAN] = (partial[n, core] + mate_part[n]).astype(BF16)
 
     others = pl.ds(0, seq_size - 1)
     pltpu.make_async_copy(xsend.at[others], xrecv.at[others], xs).wait()
     for part in range(2):
         pltpu.make_async_copy(hsend.at[part, others], hrecv.at[part, others], hs.at[part]).wait()
     pltpu.make_async_copy(ysend.at[others], yrecv.at[others], ys).wait()
-    rest = pl.ds(0, chan_size - 1)
-    pltpu.make_async_copy(gsend.at[rest], out.at[rest], gs).wait()
-
-
-def long_conv(seq_size, chan_size, value, gate_in, gate_out, skip_weight, spectrum):
+    for step in range(1, NODES):
+        pltpu.make_async_copy(gsend.at[0], grecv.at[0], gs.at[step]).wait()
+    for n in range(SPANS):
+        pltpu.make_async_copy(mate_part.at[n], mate_part.at[n], ms.at[n]).wait()
+    pass_near().wait_send()
+    pass_pair().wait_send()
+    pass_across().wait_send()
+    pass_across_pair().wait_send()
+    for slot in range(3):
+        half = weight.at[0, 0]
+        pltpu.make_async_copy(half, half, es.at[slot]).wait()
+
+
+def local(value, gate_in, gate_out, skip_weight, spectrum, out_weight):
+    seq_size = lax.axis_size("seq")
     half_rows = 8 * seq_size
     row_count = 2 * half_rows
     width = CH * seq_size
-    members = min(GROUP, seq_size)
-    groups = seq_size // members
-    krows = members * BAND
+    features = out_weight.shape[1]
+    groups = seq_size // GROUP
+    krows = GROUP * BAND
     mats = constants(seq_size)
-    skip = jnp.broadcast_to(skip_weight.reshape(seq_size, CH, 1), (seq_size, CH, LANE))
     vmem = pl.BlockSpec(memory_space=pltpu.VMEM)
+    smem = pl.BlockSpec(memory_space=pltpu.SMEM)
     hbm = pl.BlockSpec(memory_space=pl.ANY)
     dma = pltpu.SemaphoreType.DMA
     return pl.pallas_call(
-        functools.partial(conv_kernel, seq_size, chan_size),
-        out_shape=jax.ShapeDtypeStruct((chan_size, width, LANE), BF16),
-        in_specs=[vmem, vmem, hbm, vmem, hbm] + [hbm] * 5,
-        out_specs=hbm,
+        functools.partial(conv_kernel, seq_size),
+        out_shape=jax.ShapeDtypeStruct((COLS, features), BF16),
+        in_specs=[hbm, hbm, hbm, smem, hbm, hbm] + [hbm] * 5,
+        out_specs=vmem,
         scratch_shapes=[
             *[pltpu.VMEM(m.shape, F32 if m.dtype == np.float32 else BF16) for m in mats],
             pltpu.VMEM((1024, width), BF16),
+            pltpu.VMEM((1024, width), BF16),
+            pltpu.VMEM((1024, width), BF16),
             pltpu.VMEM((2, BAND, COLS, width), F32),
+            pltpu.VMEM((NODES, 2, width // 2, features), BF16),
             pltpu.VMEM((seq_size, 64, LANE), BF16),
             pltpu.VMEM((seq_size, 64, LANE), BF16),
             pltpu.VMEM((seq_size * 64, LANE), F32),
@@ -327,9 +427,11 @@
             pltpu.VMEM((seq_size, 64, LANE), BF16),
             pltpu.VMEM((seq_size, 64, LANE), BF16),
             pltpu.VMEM((seq_size * 64, LANE), F32),
-            pltpu.VMEM((8, width, LANE), BF16),
-            pltpu.VMEM((8, width, LANE), BF16),
-            dma((6,)),
+            pltpu.VMEM((NODES, 2, COLS, width), BF16),
+            pltpu.VMEM((NODES, 2, COLS, width), BF16),
+            pltpu.VMEM((SPANS, 2, COLS, SPAN), F32),
+            pltpu.VMEM((SPANS, COLS, SPAN), F32),
+            dma((9,)),
             dma((2,)),
             dma,
             dma,
@@ -337,24 +439,28 @@
             dma((2, groups)),
             dma,
             dma,
-            dma,
-            dma,
+            dma((NODES,)),
+            dma((NODES,)),
+            dma((4,)),
+            dma((4,)),
+            dma((3,)),
+            dma((3,)),
+            dma((SPANS,)),
+            dma((SPANS,)),
         ],
         compiler_params=pltpu.CompilerParams(
-            collective_id=0, has_side_effects=True, vmem_limit_bytes=50 * 1024 * 1024
+            collective_id=0, has_side_effects=True, vmem_limit_bytes=60 * 1024 * 1024
         ),
         name="long_conv",
-    )(value, gate_in, gate_out, skip, spectrum, *[jnp.asarray(m) for m in mats])
-
-
-def local(value, gate_in, gate_out, skip_weight, spectrum, out_weight):
-    seq_size = lax.axis_size("seq")
-    chan_size = lax.axis_size("chan")
-    weight = lax.all_gather(out_weight, "chan", axis=0, tiled=True)
-    gated = long_conv(seq_size, chan_size, value, gate_in, gate_out, skip_weight, spectrum)
-    gated = gated.reshape(-1, LANE)
-    out = lax.dot_general(gated, weight, (((0,), (0,)), ((), ())), preferred_element_type=F32)
-    return out.astype(BF16)
+    )(
+        value,
+        gate_in,
+        gate_out,
+        skip_weight,
+        spectrum,
+        out_weight.reshape(2, width // 2, features),
+        *[jnp.asarray(m) for m in mats],
+    )
 
 
 def solution(mesh):

time: 154 us -> 90.9 us (0.59)
  Pallas kernels: 127 us -> 88.8 us
  between operations: 13.4 us -> 0.01 us
  matrix products: 5.46 us -> 0 us
  local copies, waits for them, and re-layouts: 6.92 us -> 1.88 us
    pallas_call x1, Pallas kernels: 127 us -> 88.8 us  [local(): pl.pallas_call(functools.partial(conv_kernel, seq_size), out_shape=jax.Sh...]
    dot_general x1 -> x0, matrix products: 5.46 us -> none  [local(): lax.dot_general(gated, weight, (((0,), (0,)), ((), ())), preferred_elemen...]
    unnamed x12 -> x1, local copies, waits for them, and re-layouts: 6.06 us -> 1.88 us
  transfers between devices with their start and end apart: 1 -> 0, of which waited for: 0 -> 0; matrix products, arithmetic and copies ran while one was open for 1% -> 0% of each run, Pallas kernels for 83% -> 0%
where the time goes in v1:
time: 90.9 us; the launch traced here: 90.7 us
  Pallas kernels  88.8 us (98%)
  local copies, waits for them, and re-layouts  1.88 us (2%)
    pallas_call x1, Pallas kernels, local(): pl.pallas_call(functools.partial(conv_kernel, seq_size), out_shape=jax.Sh...  88.8 us
    unnamed x1, local copies, waits for them, and re-layouts  1.88 us

profile of v1, /device:TPU:1, one launch (start us, length us, event | category | flops | bytes accessed | tf_op | source)
XLA Modules:
  0.0 90.7 jit_solution(15736068815098644439)
XLA Ops:
  0.0 88.8 %long_conv.1 = bf16[128,2048]{1,0:T(8,128)(2,1)} custom-call(bf16[1024,256]{1,0:T(8,128)(2,1)} %value_hbm.1, bf16[1024,256]{1,0:T(8,128)(2,1)} %gate_in_hbm.1, bf16[1024,256]{1,0:T(8,128)(2,1)} %gate_out_hbm.1, f32[256]{0:T(256)} %skip.1, f32[2,16,128,256]{3,2,1,0:T(8,128)} %spectrum.1, bf16[2,128,2048]{2,1,0:T(8,128)(2,1)} %bitcast.1, ...), custom_call_target="tpu_custom_call" | custom-call | tf_op jit(solution)/shard_map/long_conv/pallas_call | solution.py:405
  88.9 1.9 %copy.13 = bf16[128,2048]{1,0:T(8,128)(2,1)} copy(bf16[128,2048]{1,0:T(8,128)(2,1)} %long_conv.1) | data formatting | bytes 1048576

commit v2 on v1

--- a/solution.py
+++ b/solution.py
@@ -16,6 +16,7 @@
 BAND = 16
 GROUP = 8
 NODES = 4
+QUARTERS = 4
 SPANS, SPAN = 4, 512
 MESH = pl.DeviceIdType.MESH
 F32 = jnp.float32
@@ -126,7 +127,7 @@
     near = lax.rem(node + 3 + 2 * low, NODES)
     far = lax.rem(node + 5 - 2 * low, NODES)
     across = lax.rem(node + 2, NODES)
-    mine = lax.rem(px + py, 2)
+    mine = lax.rem(px + 2 * py, QUARTERS)
     beside = [
         lax.rem(px + 1, 4) * 8 + py * 2 + low,
         lax.rem(px + 3, 4) * 8 + py * 2 + low,
@@ -193,41 +194,55 @@
 
         lax.fori_loop(1, seq_size, send, 0)
 
-    def pass_near():
-        block = weight.at[node, mine]
-        return remote(block, block, ws.at[0], wr.at[0], pair_chip, near * 2 + core)
+    def pass_near(step):
+        block = weight.at[node, lax.rem(mine + step, QUARTERS)]
+        sem = min(step, 1)
+        return remote(block, block, ws.at[sem], wr.at[sem], pair_chip, near * 2 + core)
 
     def pass_pair():
         block = weight.at[near, mine]
-        return remote(block, block, ws.at[1], wr.at[1], pair_chip, mc)
+        return remote(block, block, ws.at[2], wr.at[2], pair_chip, mc)
 
     def pass_across():
-        block = weight.at[far, mine, pl.ds(pl.multiple_of(low * 64, 64), 64)]
-        return remote(block, block, ws.at[2], wr.at[2], pair_chip, near * 2 + core)
+        block = weight.at[far, mine, pl.ds(pl.multiple_of(low * 32, 32), 32)]
+        return remote(block, block, ws.at[3], wr.at[3], pair_chip, near * 2 + core)
 
     def pass_across_pair():
-        block = weight.at[across, mine, pl.ds(pl.multiple_of(64 - low * 64, 64), 64)]
-        return remote(block, block, ws.at[3], wr.at[3], pair_chip, mc)
+        block = weight.at[across, mine, pl.ds(pl.multiple_of(32 - low * 32, 32), 32)]
+        return remote(block, block, ws.at[4], wr.at[4], pair_chip, mc)
 
     def pass_beside(slot, which):
         for e, seq in enumerate(beside):
-            block = weight.at[which, mine, pl.ds(e * 32, 32)]
+            rows = pl.ds(0, 64) if e < 2 else pl.ds((e - 2) * 32, 32)
+            block = weight.at[which, mine, rows]
             remote(block, block, es.at[slot], er.at[slot], seq, mc).start()
+
+    def channel(dest, c):
+        return (c // 4) * (width // 2) + dest * 4 + c % 4
 
     for copy in mixed_loads:
         copy.wait()
-    for pair in range(4):
-        halves = []
-        for a in (2 * pair, 2 * pair + 1):
-            rows = slice(a * COLS, (a + 1) * COLS)
-            mixed = (gate_in[rows, :].astype(F32) * value[rows, :].astype(F32)).astype(BF16)
-            halves.append(mixed.astype(F32).T.reshape(seq_size, CH, LANE))
-        xsend[:, pair * 16 : (pair + 1) * 16, :] = jnp.concatenate(halves, axis=1).astype(BF16)
+    for a in range(8):
+        rows = slice(a * COLS, (a + 1) * COLS)
+        mixed = (gate_in[rows, :].astype(F32) * value[rows, :].astype(F32)).astype(BF16)
+        xwide[a * width : (a + 1) * width, :] = mixed.astype(F32).T
+
+    def pack_input(dest, _):
+        for pair in range(CH // 2):
+            rows = [
+                xwide[pl.ds(channel(dest, c), 8, stride=width), :] for c in (2 * pair, 2 * pair + 1)
+            ]
+            xsend[dest, pair * 16 : (pair + 1) * 16, :] = jnp.concatenate(rows).astype(BF16)
+        return 0
+
+    lax.fori_loop(0, seq_size, pack_input, 0)
 
     weight_load.wait()
     pl.semaphore_wait(barrier, seq_size - 1 + 5)
-    pass_near().start()
+    pass_near(0).start()
     exchange(lambda peer: xsend.at[peer], xrecv.at[me], xs, xr)
+    for step in range(1, QUARTERS):
+        pass_near(step).start()
 
     for part in range(2):
         spec_loads[part].wait()
@@ -241,7 +256,7 @@
 
         def pack(dest, _):
             for c in range(CH):
-                rows = hwide[pl.ds(dest * CH + c, BAND, stride=width), :]
+                rows = hwide[pl.ds(channel(dest, c), BAND, stride=width), :]
                 hsend[part, dest, c * BAND : (c + 1) * BAND, :] = rows.astype(BF16)
             return 0
 
@@ -252,15 +267,20 @@
             hs.at[part],
             hr.at[part, px],
         )
+        if part == 0:
+            pass_near(0).wait_recv()
+            pass_pair().start()
 
     for copy in loads:
         copy.wait()
     pltpu.make_async_copy(xsend, xrecv, xr).wait()
-    pass_near().wait_recv()
-    pass_pair().start()
-    xwide[...] = xrecv[...].astype(F32).reshape(seq_size * 64, LANE)
     for c in range(CH):
-        xgrid[:, c * LANE : (c + 1) * LANE] = xwide[pl.ds(c, half_rows, stride=CH), :].astype(BF16)
+        pair = xrecv[:, c // 2 * 16 : c // 2 * 16 + 16, :].astype(F32)
+        rows = pair[:, c % 2 * 8 : c % 2 * 8 + 8, :].reshape(half_rows, LANE)
+        xgrid[:, c * LANE : (c + 1) * LANE] = rows.astype(BF16)
+    pass_pair().wait_recv()
+    pass_across().start()
+    pass_beside(0, far)
 
     def forward(g, _):
         rows = pl.ds(pl.multiple_of(g * krows, krows), krows)
@@ -282,22 +302,21 @@
         return 0
 
     lax.fori_loop(0, groups, forward, 0)
-    pass_pair().wait_recv()
-    pass_across().start()
-    pass_beside(0, near)
-    pass_beside(1, far)
+    pass_across().wait_recv()
+    pass_across_pair().start()
 
     total[...] = jnp.zeros_like(total)
 
-    def inverse(step, _):
+    def inverse(step, channels):
         g = lax.rem(px + groups - step, groups)
         members_at = pl.ds(pl.multiple_of(g * members, members), members)
-        for part in range(2):
-            block = hrecv.at[part, members_at]
-            pltpu.make_async_copy(hsend.at[part, members_at], block, hr.at[part, g]).wait()
+        if 0 in channels:
+            for part in range(2):
+                block = hrecv.at[part, members_at]
+                pltpu.make_async_copy(hsend.at[part, members_at], block, hr.at[part, g]).wait()
         rows = pl.ds(pl.multiple_of(g * krows, krows), krows)
         cos, sin = turn[0, rows, :], turn[1, rows, :]
-        for c in range(CH):
+        for c in channels:
             band = slice(c * BAND, (c + 1) * BAND)
             h_re = hrecv[0, members_at, band, :].astype(F32).reshape(krows, LANE)
             h_im = hrecv[1, members_at, band, :].astype(F32).reshape(krows, LANE)
@@ -309,64 +328,90 @@
             lanes = slice(c * LANE, (c + 1) * LANE)
             back[:krows, lanes] = (b_re * cos - b_im * sin).astype(BF16)
             back[krows:, lanes] = (b_re * sin + b_im * cos).astype(BF16)
-        for pair in range(CH // 2):
+        for pair in range(channels[0] // 2, channels[-1] // 2 + 1):
             lanes = slice(pair * 256, (pair + 1) * 256)
             total[:, lanes] += mm(inv_row[0, g], back[:, lanes]) + mm(inv_row[1, g], back[:, lanes])
+
+    def inverse_all(step, _):
+        inverse(step, range(CH))
         return 0
 
-    lax.fori_loop(0, groups - 1, inverse, 0)
-    pass_across().wait_recv()
-    pass_across_pair().start()
-    inverse(groups - 1, 0)
-
-    for pair in range(CH // 2):
-        halves = []
-        for c in (2 * pair, 2 * pair + 1):
-            lanes = slice(c * LANE, (c + 1) * LANE)
-            inner = total[:, lanes] + skip[me * CH + c] * xgrid[:, lanes].astype(F32)
-            halves.append(inner.reshape(seq_size, 8, LANE))
-        ysend[:, pair * 16 : (pair + 1) * 16, :] = jnp.concatenate(halves, axis=1).astype(BF16)
-    exchange(lambda peer: ysend.at[peer], yrecv.at[me], ys, yr)
+    lax.fori_loop(0, groups - 1, inverse_all, 0)
+
+    for part in range(2):
+        inverse(groups - 1, range(part * 4, part * 4 + 4))
+        for pair in range(2):
+            halves = []
+            for c in (part * 4 + 2 * pair, part * 4 + 2 * pair + 1):
+                lanes = slice(c * LANE, (c + 1) * LANE)
+                direct = skip[channel(me, c)] * xgrid[:, lanes].astype(F32)
+                halves.append((total[:, lanes] + direct).reshape(seq_size, 8, LANE))
+            rows = slice(pair * 16, (pair + 1) * 16)
+            ysend[part, :, rows, :] = jnp.concatenate(halves, axis=1).astype(BF16)
+        exchange(
+            lambda peer: ysend.at[part, peer], yrecv.at[part, me], ys.at[part], yr.at[part]
+        )
+
+    for part in range(2):
+        pltpu.make_async_copy(ysend.at[part], yrecv.at[part], yr.at[part]).wait()
+        ywide[...] = yrecv[part].astype(F32).reshape(seq_size * 32, LANE)
+        for step in (2, 1, 3, 0):
+            dest = lax.rem(node + step, NODES)
+            for h in range(2):
+                a = dest * 2 + h
+                inner = ywide[pl.ds(a, width // 2, stride=8), :].T
+                gate = gate_out[
+                    pl.ds(pl.multiple_of(a * COLS, COLS), COLS), part * LANE : (part + 1) * LANE
+                ]
+                gsend[part, dest, h] = (gate.astype(F32) * inner).astype(BF16)
+            if step:
+                remote(
+                    gsend.at[part, dest],
+                    grecv.at[part, node],
+                    gs.at[part, step],
+                    gr.at[part, node],
+                    me,
+                    dest * 2 + core,
+                ).start()
     pass_across_pair().wait_recv()
-    pass_beside(2, across)
-    pltpu.make_async_copy(ysend, yrecv, yr).wait()
-    ywide[...] = yrecv[...].astype(F32).reshape(seq_size * 64, LANE)
-
-    for step in (2, 1, 3, 0):
-        dest = lax.rem(node + step, NODES)
-        for h in range(2):
-            a = dest * 2 + h
-            inner = ywide[pl.ds(a, width, stride=8), :].T
-            gate = gate_out[pl.ds(pl.multiple_of(a * COLS, COLS), COLS), :]
-            gsend[dest, h] = (gate.astype(F32) * inner).astype(BF16)
-        if step:
-            remote(
-                gsend.at[dest], grecv.at[node], gs.at[step], gr.at[node], me, dest * 2 + core
-            ).start()
-
-    def product(rows_of, which, n):
-        rows = rows_of.reshape(2 * COLS, width)
+    pass_beside(1, across)
+
+    def product(sources, n):
         lanes = slice(n * SPAN, (n + 1) * SPAN)
-        return mm(rows, weight[which, :, :, lanes].reshape(width, SPAN)).reshape(2, COLS, SPAN)
+        rows = jnp.concatenate([r.reshape(2 * COLS, LANE) for r, _, _ in sources], axis=1)
+        block = jnp.concatenate(
+            [weight[w, 2 * p : 2 * p + 2, :, lanes].reshape(LANE, SPAN) for _, w, p in sources]
+        )
+        return mm(rows, block).reshape(2, COLS, SPAN)
+
+    def arrive(part, which):
+        pltpu.make_async_copy(
+            gsend.at[part, which], grecv.at[part, which], gr.at[part, which]
+        ).wait()
 
     for n in range(SPANS):
-        partial[n] = product(gsend[node], node, n)
-    for slot, which in enumerate((near, far, across)):
-        pltpu.make_async_copy(gsend.at[which], grecv.at[which], gr.at[which]).wait()
-        half = weight.at[which, 1 - mine]
-        pltpu.make_async_copy(half, half, er.at[slot]).wait()
-        rows = grecv[which]
+        partial[n] = product([(gsend[p, node], node, p) for p in range(2)], n)
+    rest = weight.at[near, pl.ds(0, QUARTERS - 1)]
+    pltpu.make_async_copy(rest, rest, wr.at[1]).wait()
+    pltpu.make_async_copy(rest, rest, er.at[0]).wait()
+    for part in range(2):
+        arrive(part, near)
+        arrive(part, far)
         for n in range(SPANS):
-            partial[n] += product(rows, which, n)
-            if slot == 2:
-                remote(
-                    partial.at[n, 1 - core],
-                    mate_part.at[n],
-                    ms.at[n],
-                    mr.at[n],
-                    me,
-                    mc + 1 - 2 * core,
-                ).start()
+            partial[n] += product([(grecv[part, w], w, part) for w in (near, far)], n)
+    pltpu.make_async_copy(rest, rest, er.at[1]).wait()
+    for part in range(2):
+        arrive(part, across)
+    for n in range(SPANS):
+        partial[n] += product([(grecv[p, across], across, p) for p in range(2)], n)
+        remote(
+            partial.at[n, 1 - core],
+            mate_part.at[n],
+            ms.at[n],
+            mr.at[n],
+            me,
+            mc + 1 - 2 * core,
+        ).start()
     for n in range(SPANS):
         pltpu.make_async_copy(mate_part.at[n], mate_part.at[n], mr.at[n]).wait()
         out[:, n * SPAN : (n + 1) * SPAN] = (partial[n, core] + mate_part[n]).astype(BF16)
@@ -375,18 +420,19 @@
     pltpu.make_async_copy(xsend.at[others], xrecv.at[others], xs).wait()
     for part in range(2):
         pltpu.make_async_copy(hsend.at[part, others], hrecv.at[part, others], hs.at[part]).wait()
-    pltpu.make_async_copy(ysend.at[others], yrecv.at[others], ys).wait()
-    for step in range(1, NODES):
-        pltpu.make_async_copy(gsend.at[0], grecv.at[0], gs.at[step]).wait()
+    for part in range(2):
+        pltpu.make_async_copy(ysend.at[part, others], yrecv.at[part, others], ys.at[part]).wait()
+        for step in range(1, NODES):
+            pltpu.make_async_copy(gsend.at[0, 0], grecv.at[0, 0], gs.at[part, step]).wait()
     for n in range(SPANS):
         pltpu.make_async_copy(mate_part.at[n], mate_part.at[n], ms.at[n]).wait()
-    pass_near().wait_send()
+    pass_near(0).wait_send()
+    pltpu.make_async_copy(rest, rest, ws.at[1]).wait()
     pass_pair().wait_send()
     pass_across().wait_send()
     pass_across_pair().wait_send()
-    for slot in range(3):
-        half = weight.at[0, 0]
-        pltpu.make_async_copy(half, half, es.at[slot]).wait()
+    for slot in range(2):
+        pltpu.make_async_copy(rest, rest, es.at[slot]).wait()
 
 
 def local(value, gate_in, gate_out, skip_weight, spectrum, out_weight):
@@ -413,7 +459,7 @@
             pltpu.VMEM((1024, width), BF16),
             pltpu.VMEM((1024, width), BF16),
             pltpu.VMEM((2, BAND, COLS, width), F32),
-            pltpu.VMEM((NODES, 2, width // 2, features), BF16),
+            pltpu.VMEM((NODES, QUARTERS, width // QUARTERS, features), BF16),
             pltpu.VMEM((seq_size, 64, LANE), BF16),
             pltpu.VMEM((seq_size, 64, LANE), BF16),
             pltpu.VMEM((seq_size * 64, LANE), F32),
@@ -424,11 +470,11 @@
             pltpu.VMEM((CH, row_count, 2 * LANE), F32),
             pltpu.VMEM((2 * krows, CH * LANE), BF16),
             pltpu.VMEM((half_rows, CH * LANE), F32),
-            pltpu.VMEM((seq_size, 64, LANE), BF16),
-            pltpu.VMEM((seq_size, 64, LANE), BF16),
-            pltpu.VMEM((seq_size * 64, LANE), F32),
-            pltpu.VMEM((NODES, 2, COLS, width), BF16),
-            pltpu.VMEM((NODES, 2, COLS, width), BF16),
+            pltpu.VMEM((2, seq_size, 32, LANE), BF16),
+            pltpu.VMEM((2, seq_size, 32, LANE), BF16),
+            pltpu.VMEM((seq_size * 32, LANE), F32),
+            pltpu.VMEM((2, NODES, 2, COLS, LANE), BF16),
+            pltpu.VMEM((2, NODES, 2, COLS, LANE), BF16),
             pltpu.VMEM((SPANS, 2, COLS, SPAN), F32),
             pltpu.VMEM((SPANS, COLS, SPAN), F32),
             dma((9,)),
@@ -437,14 +483,14 @@
             dma,
             dma((2,)),
             dma((2, groups)),
-            dma,
-            dma,
-            dma((NODES,)),
-            dma((NODES,)),
-            dma((4,)),
-            dma((4,)),
-            dma((3,)),
-            dma((3,)),
+            dma((2,)),
+            dma((2,)),
+            dma((2, NODES)),
+            dma((2, NODES)),
+            dma((5,)),
+            dma((5,)),
+            dma((2,)),
+            dma((2,)),
             dma((SPANS,)),
             dma((SPANS,)),
         ],
@@ -458,7 +504,7 @@
         gate_out,
         skip_weight,
         spectrum,
-        out_weight.reshape(2, width // 2, features),
+        out_weight.reshape(QUARTERS, width // QUARTERS, features),
         *[jnp.asarray(m) for m in mats],
     )
 

time: 90.9 us -> 75.4 us (0.83)
  Pallas kernels: 88.8 us -> 73.4 us
    pallas_call x1, Pallas kernels: 88.8 us -> 73.4 us  [local(): pl.pallas_call(functools.partial(conv_kernel, seq_size), out_shape=jax.Sh...]
where the time goes in v2:
time: 75.4 us; the launch traced here: 75.3 us
  Pallas kernels  73.4 us (97%)
  local copies, waits for them, and re-layouts  1.88 us (2%)
    pallas_call x1, Pallas kernels, local(): pl.pallas_call(functools.partial(conv_kernel, seq_size), out_shape=jax.Sh...  73.4 us
    unnamed x1, local copies, waits for them, and re-layouts  1.88 us

profile of v2, /device:TPU:1, one launch (start us, length us, event | category | flops | bytes accessed | tf_op | source)
XLA Modules:
  0.0 75.3 jit_solution(463676176156841682)
XLA Ops:
  0.0 73.4 %long_conv.1 = bf16[128,2048]{1,0:T(8,128)(2,1)} custom-call(bf16[1024,256]{1,0:T(8,128)(2,1)} %value_hbm.1, bf16[1024,256]{1,0:T(8,128)(2,1)} %gate_in_hbm.1, bf16[1024,256]{1,0:T(8,128)(2,1)} %gate_out_hbm.1, f32[256]{0:T(256)} %skip.1, f32[2,16,128,256]{3,2,1,0:T(8,128)} %spectrum.1, bf16[4,64,2048]{2,1,0:T(8,128)(2,1)} %bitcast.1, ...), custom_call_target="tpu_custom_call" | custom-call | tf_op jit(solution)/shard_map/long_conv/pallas_call | solution.py:451
  73.4 1.9 %copy.13 = bf16[128,2048]{1,0:T(8,128)(2,1)} copy(bf16[128,2048]{1,0:T(8,128)(2,1)} %long_conv.1) | data formatting | bytes 1048576

commit v3 on v2

--- a/solution.py
+++ b/solution.py
@@ -95,7 +95,6 @@
     gsend,
     grecv,
     partial,
-    mate_part,
     load_sem,
     spec_sem,
     xs,
@@ -110,8 +109,8 @@
     wr,
     es,
     er,
-    ms,
-    mr,
+    cs,
+    cr,
 ):
     me = lax.axis_index("seq")
     mc = lax.axis_index("chan")
@@ -149,7 +148,7 @@
         pltpu.make_async_copy(value_hbm, value, load_sem.at[6]),
         pltpu.make_async_copy(gate_in_hbm, gate_in, load_sem.at[7]),
     ]
-    weight_load = pltpu.make_async_copy(weight_hbm, weight.at[node], load_sem.at[8])
+    weight_load = pltpu.make_async_copy(weight_hbm, weight.at[core, node], load_sem.at[8])
     loads = [
         pltpu.make_async_copy(fwd_row_hbm, fwd_row, load_sem.at[0]),
         pltpu.make_async_copy(turn_hbm, turn, load_sem.at[1]),
@@ -175,10 +174,9 @@
         return 0
 
     lax.fori_loop(1, seq_size, greet_seq, 0)
-    greet(me, mc + 1 - 2 * core)
     greet(pair_chip, near * 2 + core)
-    for step in range(1, NODES):
-        greet(me, lax.rem(node + step, NODES) * 2 + core)
+    for step in range(1, 2 * NODES):
+        greet(me, lax.rem(mc + step, 2 * NODES))
 
     def exchange(src_of, dst, send_sem, recv_sem):
         pltpu.make_async_copy(src_of(me), dst, recv_sem).start()
@@ -195,27 +193,27 @@
         lax.fori_loop(1, seq_size, send, 0)
 
     def pass_near(step):
-        block = weight.at[node, lax.rem(mine + step, QUARTERS)]
+        block = weight.at[core, node, lax.rem(mine + step, QUARTERS)]
         sem = min(step, 1)
         return remote(block, block, ws.at[sem], wr.at[sem], pair_chip, near * 2 + core)
 
     def pass_pair():
-        block = weight.at[near, mine]
+        block = weight.at[core, near, mine]
         return remote(block, block, ws.at[2], wr.at[2], pair_chip, mc)
 
     def pass_across():
-        block = weight.at[far, mine, pl.ds(pl.multiple_of(low * 32, 32), 32)]
+        block = weight.at[core, far, mine]
         return remote(block, block, ws.at[3], wr.at[3], pair_chip, near * 2 + core)
-
-    def pass_across_pair():
-        block = weight.at[across, mine, pl.ds(pl.multiple_of(32 - low * 32, 32), 32)]
-        return remote(block, block, ws.at[4], wr.at[4], pair_chip, mc)
 
     def pass_beside(slot, which):
         for e, seq in enumerate(beside):
             rows = pl.ds(0, 64) if e < 2 else pl.ds((e - 2) * 32, 32)
-            block = weight.at[which, mine, rows]
+            block = weight.at[core, which, mine, rows]
             remote(block, block, es.at[slot], er.at[slot], seq, mc).start()
+
+    def hand_over(slot, which):
+        block = weight.at[core, which]
+        return remote(block, block, cs.at[slot], cr.at[slot], me, mc + 1 - 2 * core)
 
     def channel(dest, c):
         return (c // 4) * (width // 2) + dest * 4 + c % 4
@@ -238,11 +236,12 @@
     lax.fori_loop(0, seq_size, pack_input, 0)
 
     weight_load.wait()
-    pl.semaphore_wait(barrier, seq_size - 1 + 5)
+    pl.semaphore_wait(barrier, seq_size - 1 + 2 * NODES)
     pass_near(0).start()
     exchange(lambda peer: xsend.at[peer], xrecv.at[me], xs, xr)
     for step in range(1, QUARTERS):
         pass_near(step).start()
+    hand_over(0, node).start()
 
     for part in range(2):
         spec_loads[part].wait()
@@ -302,9 +301,6 @@
         return 0
 
     lax.fori_loop(0, groups, forward, 0)
-    pass_across().wait_recv()
-    pass_across_pair().start()
-
     total[...] = jnp.zeros_like(total)
 
     def inverse(step, channels):
@@ -364,57 +360,72 @@
                     pl.ds(pl.multiple_of(a * COLS, COLS), COLS), part * LANE : (part + 1) * LANE
                 ]
                 gsend[part, dest, h] = (gate.astype(F32) * inner).astype(BF16)
-            if step:
-                remote(
-                    gsend.at[part, dest],
-                    grecv.at[part, node],
-                    gs.at[part, step],
-                    gr.at[part, node],
-                    me,
-                    dest * 2 + core,
-                ).start()
-    pass_across_pair().wait_recv()
+                if step:
+                    remote(
+                        gsend.at[part, dest, h],
+                        grecv.at[part, node, core],
+                        gs.at[part, step * 2 + h],
+                        gr.at[part, node, core],
+                        me,
+                        dest * 2 + h,
+                    ).start()
+        own = gsend.at[part, node, core]
+        pltpu.make_async_copy(own, grecv.at[part, node, core], gr.at[part, node, core]).start()
+        remote(
+            gsend.at[part, node, 1 - core],
+            grecv.at[part, node, core],
+            gs.at[part, 0],
+            gr.at[part, node, core],
+            me,
+            mc + 1 - 2 * core,
+        ).start()
+        if part == 0:
+            rest = weight.at[core, near, pl.ds(0, QUARTERS - 1)]
+            pltpu.make_async_copy(rest, rest, wr.at[1]).wait()
+            hand_over(1, near).start()
+            pltpu.make_async_copy(rest, rest, er.at[0]).wait()
+            hand_over(2, far).start()
+    pass_across().wait_recv()
     pass_beside(1, across)
 
     def product(sources, n):
         lanes = slice(n * SPAN, (n + 1) * SPAN)
-        rows = jnp.concatenate([r.reshape(2 * COLS, LANE) for r, _, _ in sources], axis=1)
+        rows = jnp.concatenate([grecv[p, w, k] for p, w in sources for k in range(2)], axis=1)
         block = jnp.concatenate(
-            [weight[w, 2 * p : 2 * p + 2, :, lanes].reshape(LANE, SPAN) for _, w, p in sources]
+            [
+                weight[k, w, 2 * p : 2 * p + 2, :, lanes].reshape(LANE, SPAN)
+                for p, w in sources
+                for k in range(2)
+            ]
         )
-        return mm(rows, block).reshape(2, COLS, SPAN)
+        return mm(rows, block)
 
     def arrive(part, which):
-        pltpu.make_async_copy(
-            gsend.at[part, which], grecv.at[part, which], gr.at[part, which]
-        ).wait()
-
+        for k in range(2):
+            block = grecv.at[part, which, k]
+            pltpu.make_async_copy(block, block, gr.at[part, which, k]).wait()
+
+    arrive(0, node)
+    arrive(1, node)
+    hand_over(0, node).wait_recv()
     for n in range(SPANS):
-        partial[n] = product([(gsend[p, node], node, p) for p in range(2)], n)
-    rest = weight.at[near, pl.ds(0, QUARTERS - 1)]
-    pltpu.make_async_copy(rest, rest, wr.at[1]).wait()
-    pltpu.make_async_copy(rest, rest, er.at[0]).wait()
+        partial[n] = product([(0, node), (1, node)], n)
+    hand_over(1, near).wait_recv()
+    hand_over(2, far).wait_recv()
     for part in range(2):
         arrive(part, near)
         arrive(part, far)
         for n in range(SPANS):
-            partial[n] += product([(grecv[part, w], w, part) for w in (near, far)], n)
-    pltpu.make_async_copy(rest, rest, er.at[1]).wait()
-    for part in range(2):
-        arrive(part, across)
+            partial[n] += product([(part, near), (part, far)], n)
+        if part == 0:
+            pltpu.make_async_copy(rest, rest, er.at[1]).wait()
+            hand_over(3, across).start()
+    hand_over(3, across).wait_recv()
+    arrive(0, across)
+    arrive(1, across)
     for n in range(SPANS):
-        partial[n] += product([(grecv[p, across], across, p) for p in range(2)], n)
-        remote(
-            partial.at[n, 1 - core],
-            mate_part.at[n],
-            ms.at[n],
-            mr.at[n],
-            me,
-            mc + 1 - 2 * core,
-        ).start()
-    for n in range(SPANS):
-        pltpu.make_async_copy(mate_part.at[n], mate_part.at[n], mr.at[n]).wait()
-        out[:, n * SPAN : (n + 1) * SPAN] = (partial[n, core] + mate_part[n]).astype(BF16)
+        lanes = slice(n * SPAN, (n + 1) * SPAN)
+        out[:, lanes] = (partial[n] + product([(0, across), (1, across)], n)).astype(BF16)
 
     others = pl.ds(0, seq_size - 1)
     pltpu.make_async_copy(xsend.at[others], xrecv.at[others], xs).wait()
@@ -422,15 +433,16 @@
         pltpu.make_async_copy(hsend.at[part, others], hrecv.at[part, others], hs.at[part]).wait()
     for part in range(2):
         pltpu.make_async_copy(ysend.at[part, others], yrecv.at[part, others], ys.at[part]).wait()
-        for step in range(1, NODES):
-            pltpu.make_async_copy(gsend.at[0, 0], grecv.at[0, 0], gs.at[part, step]).wait()
-    for n in range(SPANS):
-        pltpu.make_async_copy(mate_part.at[n], mate_part.at[n], ms.at[n]).wait()
+        for step in [0, 2, 3, 4, 5, 6, 7]:
+            pltpu.make_async_copy(
+                gsend.at[0, 0, 0], grecv.at[0, 0, 0], gs.at[part, step]
+            ).wait()
+    for slot, which in enumerate((node, near, far, across)):
+        hand_over(slot, which).wait_send()
     pass_near(0).wait_send()
     pltpu.make_async_copy(rest, rest, ws.at[1]).wait()
     pass_pair().wait_send()
     pass_across().wait_send()
-    pass_across_pair().wait_send()
     for slot in range(2):
         pltpu.make_async_copy(rest, rest, es.at[slot]).wait()
 
@@ -459,7 +471,7 @@
             pltpu.VMEM((1024, width), BF16),
             pltpu.VMEM((1024, width), BF16),
             pltpu.VMEM((2, BAND, COLS, width), F32),
-            pltpu.VMEM((NODES, QUARTERS, width // QUARTERS, features), BF16),
+            pltpu.VMEM((2, NODES, QUARTERS, width // QUARTERS, features), BF16),
             pltpu.VMEM((seq_size, 64, LANE), BF16),
             pltpu.VMEM((seq_size, 64, LANE), BF16),
             pltpu.VMEM((seq_size * 64, LANE), F32),
@@ -475,7 +487,6 @@
             pltpu.VMEM((seq_size * 32, LANE), F32),
             pltpu.VMEM((2, NODES, 2, COLS, LANE), BF16),
             pltpu.VMEM((2, NODES, 2, COLS, LANE), BF16),
-            pltpu.VMEM((SPANS, 2, COLS, SPAN), F32),
             pltpu.VMEM((SPANS, COLS, SPAN), F32),
             dma((9,)),
             dma((2,)),
@@ -485,14 +496,14 @@
             dma((2, groups)),
             dma((2,)),
             dma((2,)),
-            dma((2, NODES)),
-            dma((2, NODES)),
-            dma((5,)),
-            dma((5,)),
+            dma((2, 2 * NODES)),
+            dma((2, NODES, 2)),
+            dma((4,)),
+            dma((4,)),
             dma((2,)),
             dma((2,)),
-            dma((SPANS,)),
-            dma((SPANS,)),
+            dma((NODES,)),
+            dma((NODES,)),
         ],
         compiler_params=pltpu.CompilerParams(
             collective_id=0, has_side_effects=True, vmem_limit_bytes=60 * 1024 * 1024

time: 75.4 us -> 74.4 us (0.987)
  Pallas kernels: 73.4 us -> 72.4 us
    pallas_call x1, Pallas kernels: 73.4 us -> 72.4 us  [local(): pl.pallas_call(functools.partial(conv_kernel, seq_size), out_shape=jax.Sh...]
where the time goes in v3:
time: 74.4 us; the launch traced here: 74.3 us
  Pallas kernels  72.4 us (97%)
  local copies, waits for them, and re-layouts  1.88 us (3%)
    pallas_call x1, Pallas kernels, local(): pl.pallas_call(functools.partial(conv_kernel, seq_size), out_shape=jax.Sh...  72.4 us
    unnamed x1, local copies, waits for them, and re-layouts  1.88 us

profile of v3, /device:TPU:1, one launch (start us, length us, event | category | flops | bytes accessed | tf_op | source)
XLA Modules:
  0.0 74.3 jit_solution(15766066297303014356)
XLA Ops:
  0.0 72.4 %long_conv.1 = bf16[128,2048]{1,0:T(8,128)(2,1)} custom-call(bf16[1024,256]{1,0:T(8,128)(2,1)} %value_hbm.1, bf16[1024,256]{1,0:T(8,128)(2,1)} %gate_in_hbm.1, bf16[1024,256]{1,0:T(8,128)(2,1)} %gate_out_hbm.1, f32[256]{0:T(256)} %skip.1, f32[2,16,128,256]{3,2,1,0:T(8,128)} %spectrum.1, bf16[4,64,2048]{2,1,0:T(8,128)(2,1)} %bitcast.1, ...), custom_call_target="tpu_custom_call" | custom-call | tf_op jit(solution)/shard_map/long_conv/pallas_call | solution.py:463
  72.4 1.9 %copy.13 = bf16[128,2048]{1,0:T(8,128)(2,1)} copy(bf16[128,2048]{1,0:T(8,128)(2,1)} %long_conv.1) | data formatting | bytes 1048576

commit v4 on v3

--- a/solution.py
+++ b/solution.py
@@ -111,6 +111,8 @@
     er,
     cs,
     cr,
+    result,
+    os,
 ):
     me = lax.axis_index("seq")
     mc = lax.axis_index("chan")
@@ -385,8 +387,8 @@
             hand_over(1, near).start()
             pltpu.make_async_copy(rest, rest, er.at[0]).wait()
             hand_over(2, far).start()
-    pass_across().wait_recv()
-    pass_beside(1, across)
+            pass_across().wait_recv()
+            pass_beside(1, across)
 
     def product(sources, n):
         lanes = slice(n * SPAN, (n + 1) * SPAN)
@@ -412,20 +414,28 @@
         partial[n] = product([(0, node), (1, node)], n)
     hand_over(1, near).wait_recv()
     hand_over(2, far).wait_recv()
-    for part in range(2):
-        arrive(part, near)
-        arrive(part, far)
+    arrive(0, near)
+    arrive(0, far)
+    for n in range(SPANS):
+        partial[n] += product([(0, near), (0, far)], n)
+    pltpu.make_async_copy(rest, rest, er.at[1]).wait()
+    hand_over(3, across).start()
+    arrive(0, across)
+    hand_over(3, across).wait_recv()
+    for n in range(SPANS):
+        partial[n] += product([(0, across)], n)
+    for which in (near, far):
+        arrive(1, which)
         for n in range(SPANS):
-            partial[n] += product([(part, near), (part, far)], n)
-        if part == 0:
-            pltpu.make_async_copy(rest, rest, er.at[1]).wait()
-            hand_over(3, across).start()
-    hand_over(3, across).wait_recv()
-    arrive(0, across)
+            partial[n] += product([(1, which)], n)
     arrive(1, across)
     for n in range(SPANS):
         lanes = slice(n * SPAN, (n + 1) * SPAN)
-        out[:, lanes] = (partial[n] + product([(0, across), (1, across)], n)).astype(BF16)
+        result[:, lanes] = (partial[n] + product([(1, across)], n)).astype(BF16)
+        pltpu.make_async_copy(result.at[:, lanes], out.at[:, lanes], os.at[n]).start()
+    for n in range(SPANS):
+        lanes = slice(n * SPAN, (n + 1) * SPAN)
+        pltpu.make_async_copy(result.at[:, lanes], out.at[:, lanes], os.at[n]).wait()
 
     others = pl.ds(0, seq_size - 1)
     pltpu.make_async_copy(xsend.at[others], xrecv.at[others], xs).wait()
@@ -456,7 +466,6 @@
     groups = seq_size // GROUP
     krows = GROUP * BAND
     mats = constants(seq_size)
-    vmem = pl.BlockSpec(memory_space=pltpu.VMEM)
     smem = pl.BlockSpec(memory_space=pltpu.SMEM)
     hbm = pl.BlockSpec(memory_space=pl.ANY)
     dma = pltpu.SemaphoreType.DMA
@@ -464,7 +473,7 @@
         functools.partial(conv_kernel, seq_size),
         out_shape=jax.ShapeDtypeStruct((COLS, features), BF16),
         in_specs=[hbm, hbm, hbm, smem, hbm, hbm] + [hbm] * 5,
-        out_specs=vmem,
+        out_specs=hbm,
         scratch_shapes=[
             *[pltpu.VMEM(m.shape, F32 if m.dtype == np.float32 else BF16) for m in mats],
             pltpu.VMEM((1024, width), BF16),
@@ -504,6 +513,8 @@
             dma((2,)),
             dma((NODES,)),
             dma((NODES,)),
+            pltpu.VMEM((COLS, features), BF16),
+            dma((SPANS,)),
         ],
         compiler_params=pltpu.CompilerParams(
             collective_id=0, has_side_effects=True, vmem_limit_bytes=60 * 1024 * 1024

time: 74.4 us -> 73.7 us (level)
  Pallas kernels: 72.4 us -> 71.6 us
    pallas_call x1, Pallas kernels: 72.4 us -> 71.6 us  [local(): pl.pallas_call(functools.partial(conv_kernel, seq_size), out_shape=jax.Sh...]
where the time goes in v4:
time: 73.7 us; the launch traced here: 73.5 us
  Pallas kernels  71.6 us (97%)
  local copies, waits for them, and re-layouts  1.88 us (3%)
    pallas_call x1, Pallas kernels, local(): pl.pallas_call(functools.partial(conv_kernel, seq_size), out_shape=jax.Sh...  71.6 us
    unnamed x1, local copies, waits for them, and re-layouts  1.88 us

profile of v4, /device:TPU:1, one launch (start us, length us, event | category | flops | bytes accessed | tf_op | source)
XLA Modules:
  0.0 73.5 jit_solution(6574517147317490284)
XLA Ops:
  0.0 71.6 %long_conv.1 = bf16[128,2048]{1,0:T(8,128)(2,1)} custom-call(bf16[1024,256]{1,0:T(8,128)(2,1)} %value_hbm.1, bf16[1024,256]{1,0:T(8,128)(2,1)} %gate_in_hbm.1, bf16[1024,256]{1,0:T(8,128)(2,1)} %gate_out_hbm.1, f32[256]{0:T(256)} %skip.1, f32[2,16,128,256]{3,2,1,0:T(8,128)} %spectrum.1, bf16[4,64,2048]{2,1,0:T(8,128)(2,1)} %bitcast.1, ...), custom_call_target="tpu_custom_call" | custom-call | tf_op jit(solution)/shard_map/long_conv/pallas_call | solution.py:472
  71.7 1.9 %copy.13 = bf16[128,2048]{1,0:T(8,128)(2,1)} copy(bf16[128,2048]{1,0:T(8,128)(2,1)} %long_conv.1) | data formatting | bytes 1048576

commit v5 on v4

--- a/solution.py
+++ b/solution.py
@@ -163,7 +163,7 @@
         pltpu.make_async_copy(spectrum.at[part], spec_buf.at[part], spec_sem.at[part])
         for part in range(2)
     ]
-    for copy in mixed_loads + [weight_load] + spec_loads + loads:
+    for copy in mixed_loads:
         copy.start()
 
     barrier = pltpu.get_barrier_semaphore()
@@ -222,6 +222,8 @@
 
     for copy in mixed_loads:
         copy.wait()
+    for copy in [weight_load] + spec_loads + loads:
+        copy.start()
     for a in range(8):
         rows = slice(a * COLS, (a + 1) * COLS)
         mixed = (gate_in[rows, :].astype(F32) * value[rows, :].astype(F32)).astype(BF16)
@@ -350,10 +352,11 @@
             lambda peer: ysend.at[part, peer], yrecv.at[part, me], ys.at[part], yr.at[part]
         )
 
+    rest = weight.at[core, near, pl.ds(0, QUARTERS - 1)]
     for part in range(2):
         pltpu.make_async_copy(ysend.at[part], yrecv.at[part], yr.at[part]).wait()
-        ywide[...] = yrecv[part].astype(F32).reshape(seq_size * 32, LANE)
-        for step in (2, 1, 3, 0):
+        ywide[: seq_size * 32, :] = yrecv[part].astype(F32).reshape(seq_size * 32, LANE)
+        for step in (1, 3, 2, 0):
             dest = lax.rem(node + step, NODES)
             for h in range(2):
                 a = dest * 2 + h
@@ -382,13 +385,13 @@
             mc + 1 - 2 * core,
         ).start()
         if part == 0:
-            rest = weight.at[core, near, pl.ds(0, QUARTERS - 1)]
             pltpu.make_async_copy(rest, rest, wr.at[1]).wait()
             hand_over(1, near).start()
-            pltpu.make_async_copy(rest, rest, er.at[0]).wait()
-            hand_over(2, far).start()
             pass_across().wait_recv()
             pass_beside(1, across)
+
+    pltpu.make_async_copy(rest, rest, er.at[0]).wait()
+    hand_over(2, far).start()
 
     def product(sources, n):
         lanes = slice(n * SPAN, (n + 1) * SPAN)
@@ -483,9 +486,9 @@
             pltpu.VMEM((2, NODES, QUARTERS, width // QUARTERS, features), BF16),
             pltpu.VMEM((seq_size, 64, LANE), BF16),
             pltpu.VMEM((seq_size, 64, LANE), BF16),
-            pltpu.VMEM((seq_size * 64, LANE), F32),
+            pltpu.VMEM((seq_size * 64 + width, LANE), F32),
             pltpu.VMEM((half_rows, CH * LANE), BF16),
-            pltpu.VMEM((BAND * width, LANE), F32),
+            pltpu.VMEM(((BAND + 1) * width, LANE), F32),
             pltpu.VMEM((2, seq_size, CH * BAND, LANE), BF16),
             pltpu.VMEM((2, seq_size, CH * BAND, LANE), BF16),
             pltpu.VMEM((CH, row_count, 2 * LANE), F32),
@@ -493,7 +496,7 @@
             pltpu.VMEM((half_rows, CH * LANE), F32),
             pltpu.VMEM((2, seq_size, 32, LANE), BF16),
             pltpu.VMEM((2, seq_size, 32, LANE), BF16),
-            pltpu.VMEM((seq_size * 32, LANE), F32),
+            pltpu.VMEM((seq_size * 32 + 8, LANE), F32),
             pltpu.VMEM((2, NODES, 2, COLS, LANE), BF16),
             pltpu.VMEM((2, NODES, 2, COLS, LANE), BF16),
             pltpu.VMEM((SPANS, COLS, SPAN), F32),

time: 73.7 us -> 72 us (0.977)
  Pallas kernels: 71.6 us -> 69.9 us
    pallas_call x1, Pallas kernels: 71.6 us -> 69.9 us  [local(): pl.pallas_call(functools.partial(conv_kernel, seq_size), out_shape=jax.Sh...]
where the time goes in v5:
time: 72 us; the launch traced here: 71.8 us
  Pallas kernels  69.9 us (97%)
  local copies, waits for them, and re-layouts  1.88 us (3%)
    pallas_call x1, Pallas kernels, local(): pl.pallas_call(functools.partial(conv_kernel, seq_size), out_shape=jax.Sh...  69.9 us
    unnamed x1, local copies, waits for them, and re-layouts  1.88 us

profile of v5, /device:TPU:1, one launch (start us, length us, event | category | flops | bytes accessed | tf_op | source)
XLA Modules:
  0.0 71.8 jit_solution(11111498501836087095)
XLA Ops:
  0.0 69.9 %long_conv.1 = bf16[128,2048]{1,0:T(8,128)(2,1)} custom-call(bf16[1024,256]{1,0:T(8,128)(2,1)} %value_hbm.1, bf16[1024,256]{1,0:T(8,128)(2,1)} %gate_in_hbm.1, bf16[1024,256]{1,0:T(8,128)(2,1)} %gate_out_hbm.1, f32[256]{0:T(256)} %skip.1, f32[2,16,128,256]{3,2,1,0:T(8,128)} %spectrum.1, bf16[4,64,2048]{2,1,0:T(8,128)(2,1)} %bitcast.1, ...), custom_call_target="tpu_custom_call" | custom-call | tf_op jit(solution)/shard_map/long_conv/pallas_call | solution.py:475
  70.0 1.9 %copy.13 = bf16[128,2048]{1,0:T(8,128)(2,1)} copy(bf16[128,2048]{1,0:T(8,128)(2,1)} %long_conv.1) | data formatting | bytes 1048576

commit v6 on v5

--- a/solution.py
+++ b/solution.py
@@ -356,24 +356,23 @@
     for part in range(2):
         pltpu.make_async_copy(ysend.at[part], yrecv.at[part], yr.at[part]).wait()
         ywide[: seq_size * 32, :] = yrecv[part].astype(F32).reshape(seq_size * 32, LANE)
-        for step in (1, 3, 2, 0):
+        for step, h in ((1, 0), (3, 0), (1, 1), (3, 1), (2, 0), (2, 1), (0, 0), (0, 1)):
             dest = lax.rem(node + step, NODES)
-            for h in range(2):
-                a = dest * 2 + h
-                inner = ywide[pl.ds(a, width // 2, stride=8), :].T
-                gate = gate_out[
-                    pl.ds(pl.multiple_of(a * COLS, COLS), COLS), part * LANE : (part + 1) * LANE
-                ]
-                gsend[part, dest, h] = (gate.astype(F32) * inner).astype(BF16)
-                if step:
-                    remote(
-                        gsend.at[part, dest, h],
-                        grecv.at[part, node, core],
-                        gs.at[part, step * 2 + h],
-                        gr.at[part, node, core],
-                        me,
-                        dest * 2 + h,
-                    ).start()
+            a = dest * 2 + h
+            inner = ywide[pl.ds(a, width // 2, stride=8), :].T
+            gate = gate_out[
+                pl.ds(pl.multiple_of(a * COLS, COLS), COLS), part * LANE : (part + 1) * LANE
+            ]
+            gsend[part, dest, h] = (gate.astype(F32) * inner).astype(BF16)
+            if step:
+                remote(
+                    gsend.at[part, dest, h],
+                    grecv.at[part, node, core],
+                    gs.at[part, step * 2 + h],
+                    gr.at[part, node, core],
+                    me,
+                    dest * 2 + h,
+                ).start()
         own = gsend.at[part, node, core]
         pltpu.make_async_copy(own, grecv.at[part, node, core], gr.at[part, node, core]).start()
         remote(

time: 72 us -> 72 us (level)
  no operation moved by 1% of the time
where the time goes in v6:
time: 72 us; the launch traced here: 71.8 us
  Pallas kernels  69.9 us (97%)
  local copies, waits for them, and re-layouts  1.88 us (3%)
    pallas_call x1, Pallas kernels, local(): pl.pallas_call(functools.partial(conv_kernel, seq_size), out_shape=jax.Sh...  69.9 us
    unnamed x1, local copies, waits for them, and re-layouts  1.88 us

profile of v6, /device:TPU:1, one launch (start us, length us, event | category | flops | bytes accessed | tf_op | source)
XLA Modules:
  0.0 71.8 jit_solution(15828871413422142006)
XLA Ops:
  0.0 69.9 %long_conv.1 = bf16[128,2048]{1,0:T(8,128)(2,1)} custom-call(bf16[1024,256]{1,0:T(8,128)(2,1)} %value_hbm.1, bf16[1024,256]{1,0:T(8,128)(2,1)} %gate_in_hbm.1, bf16[1024,256]{1,0:T(8,128)(2,1)} %gate_out_hbm.1, f32[256]{0:T(256)} %skip.1, f32[2,16,128,256]{3,2,1,0:T(8,128)} %spectrum.1, bf16[4,64,2048]{2,1,0:T(8,128)(2,1)} %bitcast.1, ...), custom_call_target="tpu_custom_call" | custom-call | tf_op jit(solution)/shard_map/long_conv/pallas_call | solution.py:474
  70.0 1.9 %copy.13 = bf16[128,2048]{1,0:T(8,128)(2,1)} copy(bf16[128,2048]{1,0:T(8,128)(2,1)} %long_conv.1) | data formatting | bytes 1048576
